TPU v7x, 32 devices: a whole 2x2x4 slice. The times are simulated.
32 devices in a mesh: shot: 2 (over y), freq: 4 (over z), tile: 4 (over x, core).
Axes of the slice: x: 2, y: 2, z: 4, core: 2. Of those that a mesh axis runs over, the one named last changes fastest.
Arguments:
- omega: float32 [8], P('freq'), may hold values from 30 to 150
- wavefields: float32 [4, 2, 8, 1024, 256], P('shot', None, 'freq', 'tile'), parts along dimension 0, may hold values from -2.5 to 2.5
- velocity: float32 [2, 1024, 256], P(None, ('tile', 'freq')), may hold values from 1.5 to 4.5
- eta: float32 [2, 1024, 256], P(None, ('tile', 'freq')), may hold values from 0 to 0.3
Outputs:
- image: float32 [4, 1024, 256], P('shot', ('tile', 'freq')), parts along dimension 0
There are 2 independent parts, one for each index of `shot`. A program takes and returns all parts, laid end to end along the dimension named above; an argument that names none is the same for every part. Nothing has to cross between parts.
All inputs are finite; a program needn't handle non-finite values.
Results may differ from a plain program's by a relative error of at most 0.0001.
Values sent between devices are 32-bit elements; how exact they have to be, the bound alone decides.
A program may use at most 64 MiB of HBM per device.

v0:
```python
import jax
import jax.numpy as jnp
from jax import lax
from jax.sharding import PartitionSpec as P

coeffs = ((1, 1.5), (2, -0.15), (3, 1.0 / 90.0))
centre = -49.0 / 9.0
lateral_scale = 0.5
depth_step = 0.01


def with_halo(cells, sides, width):
    for axis, dim in sides:
        count = lax.axis_size(axis)
        ends = count - 1
        head = lax.slice_in_dim(cells, 0, width, axis=dim)
        tail = lax.slice_in_dim(cells, cells.shape[dim] - width, cells.shape[dim], axis=dim)
        cells = jnp.concatenate(
            [
                lax.ppermute(tail, axis, [(i, (i + 1) % count) for i in range(ends)]),
                cells,
                lax.ppermute(head, axis, [((i + 1) % count, i) for i in range(ends)]),
            ],
            axis=dim,
        )
    return cells


def stencil(padded):
    rows = padded.shape[-2] - 6
    cols = padded.shape[-1] - 6
    core = padded[..., 3 : 3 + rows, 3 : 3 + cols]
    total = 2.0 * centre * core
    for shift, weight in coeffs:
        part = (
            padded[..., 3 + shift : 3 + shift + rows, 3 : 3 + cols]
            + padded[..., 3 - shift : 3 - shift + rows, 3 : 3 + cols]
        )
        part = (
            part
            + padded[..., 3 : 3 + rows, 3 + shift : 3 + shift + cols]
            + padded[..., 3 : 3 + rows, 3 - shift : 3 - shift + cols]
        )
        total = total + weight * part
    return total


def advance(field, lap, vel, eta_d, om):
    signs = jnp.array([-1.0, 1.0], jnp.float32).reshape((2,) + (1,) * (field.ndim - 2))
    real_part, imag_part = (field[:, 0], field[:, 1])
    lap_re, lap_im = (lap[:, 0], lap[:, 1])
    theta = lateral_scale * vel * (1.0 + 2.0 * eta_d) / om
    v_re = real_part - signs * theta * lap_im
    v_im = imag_part + signs * theta * lap_re
    phase = om * depth_step / vel
    cosine = jnp.cos(phase)
    sine = signs * jnp.sin(phase)
    out_re = cosine * v_re - sine * v_im
    out_im = cosine * v_im + sine * v_re
    term = jnp.sum(out_re[0] * out_re[1] + out_im[0] * out_im[1], axis=0)
    return (jnp.stack([out_re, out_im], axis=1), term)


def per_device(omega, wavefields, velocity, eta):
    freq_count = omega.shape[0]
    om = omega.reshape(freq_count, 1, 1)
    field = wavefields
    images = []
    for depth in range(velocity.shape[0]):
        rimmed = with_halo(field, (("tile", 3),), 3)
        padded = jnp.pad(rimmed, ((0, 0), (0, 0), (0, 0), (0, 0), (3, 3)))
        lap = stencil(padded)
        vel, eta_d = (
            lax.all_gather(velocity[depth], "freq", axis=0, tiled=True),
            lax.all_gather(eta[depth], "freq", axis=0, tiled=True),
        )
        field, term = advance(field, lap, vel, eta_d, om)
        images.append(lax.psum_scatter(term, "freq", scatter_dimension=0, tiled=True))
    return jnp.stack(images)


def solution(mesh):
    return jax.shard_map(
        per_device,
        mesh=mesh,
        in_specs=(
            P("freq"),
            P("shot", None, "freq", "tile", None),
            P(None, ("tile", "freq"), None),
            P(None, ("tile", "freq"), None),
        ),
        out_specs=P("shot", ("tile", "freq"), None),
        check_vma=False,
    )
```

profile of v0, /device:TPU:0, one launch (start us, length us, event | category | flops | bytes accessed | tf_op | source)
XLA Modules:
  0.0 145.5 jit_solution(230321352615536012)
XLA Ops:
  6.5 0.0 copy-start.2
  6.5 0.0 reduce-scatter.5.cloned.1.call-start
  6.5 0.9 fusion.46
  7.4 1.3 collective-permute-start
  8.7 3.0 %collective-permute-start.1 = (f32[2,2,2,3,256]{4,3,2,1,0:T(4,128)S(1)}, f32[2,2,2,3,256]{4,3,2,1,0:T(4,128)S(1)}, u32[]{:S(2)}, u32[]{:S(2)}) collective-permute-start(f32[2,2,2,3,256]{4,3,2,1,0:T(4,128)S(1)} %get-tuple-element.13), channel_id=1, source_target_pairs={{0,1},{1,2},{2,3},{4,5},{5,6},{6,7},{8,9},{9,10},{10,11},{12,13},{... | collective-permute-start | bytes 73736 | tf_op jit(solution)/shard_map/ppermute | solution.py:20
  11.8 0.7 broadcast_multiply_fusion
  12.4 0.9 fusion.48
  13.3 0.9 fusion.47
  14.2 16.0 %all-gather = f32[1,256,256]{2,1,0:T(8,128)S(1)} all-gather(f32[1,64,256]{2,1,0:T(8,128)S(1)} %get-tuple-element.20), channel_id=2, replica_groups=mesh['shot'=2,'freq'=4,'tile'=4] {'freq'}, dimensions={1}, use_global_device_ids=true | all-gather | bytes 327680 | tf_op jit(solution)/shard_map/all_gather | solution.py:74
  30.2 13.8 %all-gather.3 = f32[1,256,256]{2,1,0:T(8,128)S(1)} all-gather(f32[1,64,256]{2,1,0:T(8,128)S(1)} %get-tuple-element.18), channel_id=5, replica_groups=mesh['shot'=2,'freq'=4,'tile'=4] {'freq'}, dimensions={1}, use_global_device_ids=true | all-gather | bytes 327680 | tf_op jit(solution)/shard_map/all_gather | solution.py:75
  44.1 14.2 %all-gather.2 = f32[1,256,256]{2,1,0:T(8,128)S(1)} all-gather(f32[1,64,256]{2,1,0:T(8,128)S(1)} %get-tuple-element.21), channel_id=4, replica_groups=mesh['shot'=2,'freq'=4,'tile'=4] {'freq'}, dimensions={1}, use_global_device_ids=true | all-gather | bytes 327680 | tf_op jit(solution)/shard_map/all_gather | solution.py:74
  58.3 13.8 %all-gather.1 = f32[1,256,256]{2,1,0:T(8,128)S(1)} all-gather(f32[1,64,256]{2,1,0:T(8,128)S(1)} %get-tuple-element.19), channel_id=3, replica_groups=mesh['shot'=2,'freq'=4,'tile'=4] {'freq'}, dimensions={1}, use_global_device_ids=true | all-gather | bytes 327680 | tf_op jit(solution)/shard_map/all_gather | solution.py:75
  72.2 0.0 copy-done.2
  72.2 0.0 copy-start
  72.2 0.2 broadcast_divide_fusion
  72.4 3.7 %divide_cosine_fusion.1 = (f32[2,256,256]{2,1,0:T(8,128)S(1)}, f32[2,256,256]{2,1,0:T(8,128)S(1)}, f32[2,256,256]{2,1,0:T(8,128)S(1)}, f32[2,256,256]{2,1,0:T(8,128)S(1)}) fusion(f32[256,256]{1,0:T(8,128)S(1)} %bitcast.100, f32[2]{0:T(128)S(1)} %broadcast_multiply_fusion, f32[256,256]{1,0:T(8,128)S(1)} %bitcast.101), kind=kLoop, calls=%fused_computation.92 | loop fusion | flops 262144 | bytes 2621448 | tf_op jit(solution)/shard_map/cos | solution.py:56
  76.1 0.0 copy-done
  76.1 0.2 constant_dynamic-update-slice_fusion.1
  76.3 0.0 collective-permute-done
  76.4 0.0 collective-permute-done.1
  76.4 1.0 select_maximum_fusion.3
  77.4 0.0 copy-start.1
  77.4 3.0 %fusion.11 = f32[2,2,2,256,256]{4,3,2,1,0:T(8,128)S(1)} fusion(f32[2,2,2,3,256]{4,3,2,1,0:T(4,128)S(1)} %collective-permute-done.1, f32[2,2,2,262,262]{4,3,2,1,0:T(8,128)S(1)} %select_maximum_fusion.3, f32[2,2,2,256,256]{4,3,2,1,0:T(8,128)S(1)} %copy-done, f32[2,2,2,259,256]{4,3,2,1,0:T(8,128)S(1)} %constant_dynamic-update-slice_fusion), kind=kLoop, calls=%fused_computation.27 | loop fusion | flops 9961472 | bytes 23093248 | tf_op jit(solution)/shard_map/add | solution.py:44
  80.4 0.0 copy-done.1
  80.4 0.4 fusion.33
  80.8 0.4 fusion.35
  81.3 1.3 collective-permute-start.3
  82.6 1.5 %collective-permute-start.2 = (f32[2,2,2,3,256]{4,3,2,1,0:T(4,128)S(1)}, f32[2,2,2,3,256]{4,3,2,1,0:T(4,128)S(1)}, u32[]{:S(2)}, u32[]{:S(2)}) collective-permute-start(f32[2,2,2,3,256]{4,3,2,1,0:T(4,128)S(1)} %get-tuple-element.11), channel_id=1, source_target_pairs={{1,0},{2,1},{3,2},{5,4},{6,5},{7,6},{9,8},{10,9},{11,10},{13,12},{... | collective-permute-start | bytes 73736 | tf_op jit(solution)/shard_map/ppermute | solution.py:22
  84.1 0.0 collective-permute-done.3
  84.1 3.5 %collective-permute-done.2 = f32[2,2,2,3,256]{4,3,2,1,0:T(4,128)S(1)} collective-permute-done((f32[2,2,2,3,256]{4,3,2,1,0:T(4,128)S(1)}, f32[2,2,2,3,256]{4,3,2,1,0:T(4,128)S(1)}, u32[]{:S(2)}, u32[]{:S(2)}) %collective-permute-start.2) | collective-permute-done | bytes 24608 | tf_op jit(solution)/shard_map/ppermute | solution.py:22
  87.5 1.0 select_maximum_fusion
  88.6 0.4 pad_maximum_fusion.1
  89.0 2.9 %fusion.4 = f32[2,2,2,256,256]{4,3,2,1,0:T(8,128)S(1)} fusion(f32[2,1,2,256,256]{4,3,2,1,0:T(8,128)S(1)} %fusion.35, f32[2,1,2,256,256]{4,3,2,1,0:T(8,128)S(1)} %fusion.33, f32[2,2,2,262,262]{4,3,2,1,0:T(8,128)S(1)} %select_maximum_fusion, f32[2,2,2,259,256]{4,3,2,1,0:T(8,128)S(1)} %get-tuple-element.9, f32[2,2,2,259,256]{4,3,2,1,0:T(8,128)S(1)} %get-tuple-element.8), kind=kLoop, calls=%fused_computation.20 | loop fusion | flops 8912896 | bytes 29360128 | tf_op jit(solution)/shard_map/add | solution.py:44
  91.9 0.9 fusion.36
  92.8 0.6 fusion.37
  93.4 0.8 fusion.39
  94.3 0.0 reduce-scatter.5.cloned.1.call-update
  94.3 0.0 reduce-scatter.3.cloned.1.call-start
  94.4 0.8 fusion.41
  95.2 0.0 reduce-scatter.3.cloned.1.call-update
  95.2 21.6 %reduce-scatter.5.cloned.1.call-done = f32[64,256]{1,0:T(8,128)} async-done(((f32[256,256]{1,0:T(8,128)}), f32[64,256]{1,0:T(8,128)}) %reduce-scatter.5.cloned.1.call-update) | async-done | bytes 65552 | tf_op jit(solution)/shard_map/reduce_scatter | solution.py:78
  116.8 20.2 %reduce-scatter.3.cloned.1.call-done = f32[64,256]{1,0:T(8,128)} async-done(((f32[256,256]{1,0:T(8,128)}), f32[64,256]{1,0:T(8,128)}) %reduce-scatter.3.cloned.1.call-update) | async-done | bytes 65552 | tf_op jit(solution)/shard_map/reduce_scatter | solution.py:78
  137.1 1.5 %pad_maximum_fusion.3 = f32[2,64,256]{2,1,0:T(8,128)} fusion(f32[1,64,256]{2,1,0:T(8,128)} %bitcast.102, f32[1,64,256]{2,1,0:T(8,128)} %bitcast.103), kind=kLoop, calls=%fused_computation.97 | loop fusion | flops 32768 | bytes 262144 | tf_op jit(solution)/shard_map/stack | solution.py:79
  (4 shorter events, 0.1 us)
Async XLA Ops:
  6.5 65.7 %copy-start.2 = (f32[2]{0:T(128)S(1)}, f32[2]{0:T(128)}, u32[]{:S(2)}) copy-start(f32[2]{0:T(128)} %param.6) | copy-start | bytes 28
  6.5 110.3 %reduce-scatter.5.cloned.1.call-start = ((), (), s32[]{:S(2)}) async-start(), calls=%async_computation.3 | async-start | bytes 327680 | tf_op jit(solution)/shard_map/reduce_scatter | solution.py:78
  7.4 68.9 %collective-permute-start = (f32[2,2,2,3,256]{4,3,2,1,0:T(4,128)S(1)}, f32[2,2,2,3,256]{4,3,2,1,0:T(4,128)S(1)}, u32[]{:S(2)}, u32[]{:S(2)}) collective-permute-start(f32[2,2,2,3,256]{4,3,2,1,0:T(4,128)S(1)} %get-tuple-element.12), channel_id=1, source_target_pairs={{1,0},{2,1},{3,2},{5,4},{6,5},{7,6},{9,8},{10,9},{11,10},{13,12},{... | collective-permute-start | bytes 73736 | tf_op jit(solution)/shard_map/ppermute | solution.py:22
  8.7 67.6 %collective-permute-start.1 = (f32[2,2,2,3,256]{4,3,2,1,0:T(4,128)S(1)}, f32[2,2,2,3,256]{4,3,2,1,0:T(4,128)S(1)}, u32[]{:S(2)}, u32[]{:S(2)}) collective-permute-start(f32[2,2,2,3,256]{4,3,2,1,0:T(4,128)S(1)} %get-tuple-element.13), channel_id=1, source_target_pairs={{0,1},{1,2},{2,3},{4,5},{5,6},{6,7},{8,9},{9,10},{10,11},{12,13},{... | collective-permute-start | bytes 73736 | tf_op jit(solution)/shard_map/ppermute | solution.py:20
  72.2 3.9 %copy-start = (f32[2,2,2,256,256]{4,3,2,1,0:T(8,128)S(1)}, f32[2,2,2,256,256]{4,3,2,1,0:T(8,128)}, u32[]{:S(2)}) copy-start(f32[2,2,2,256,256]{4,3,2,1,0:T(8,128)} %param.7) | copy-start | bytes 6291460
  77.4 3.0 %copy-start.1 = (f32[2]{0:T(128)S(1)}, f32[2]{0:T(128)}, u32[]{:S(2)}) copy-start(f32[2]{0:T(128)} %constant.22.clone) | copy-start | bytes 28
  81.3 2.8 %collective-permute-start.3 = (f32[2,2,2,3,256]{4,3,2,1,0:T(4,128)S(1)}, f32[2,2,2,3,256]{4,3,2,1,0:T(4,128)S(1)}, u32[]{:S(2)}, u32[]{:S(2)}) collective-permute-start(f32[2,2,2,3,256]{4,3,2,1,0:T(4,128)S(1)} %get-tuple-element.10), channel_id=1, source_target_pairs={{0,1},{1,2},{2,3},{4,5},{5,6},{6,7},{8,9},{9,10},{10,11},{12,13},{... | collective-permute-start | bytes 73736 | tf_op jit(solution)/shard_map/ppermute | solution.py:20
  82.6 4.9 %collective-permute-start.2 = (f32[2,2,2,3,256]{4,3,2,1,0:T(4,128)S(1)}, f32[2,2,2,3,256]{4,3,2,1,0:T(4,128)S(1)}, u32[]{:S(2)}, u32[]{:S(2)}) collective-permute-start(f32[2,2,2,3,256]{4,3,2,1,0:T(4,128)S(1)} %get-tuple-element.11), channel_id=1, source_target_pairs={{1,0},{2,1},{3,2},{5,4},{6,5},{7,6},{9,8},{10,9},{11,10},{13,12},{... | collective-permute-start | bytes 73736 | tf_op jit(solution)/shard_map/ppermute | solution.py:22
  94.3 42.8 %reduce-scatter.3.cloned.1.call-start = ((), (), s32[]{:S(2)}) async-start(), calls=%async_computation.2 | async-start | bytes 327680 | tf_op jit(solution)/shard_map/reduce_scatter | solution.py:78
Sparse Core Ops, SparseCore 0:
  94.4 22.3 reduce-scatter.4
  119.2 17.8 reduce-scatter.2
where the time goes:
time: 146 us; the launch traced here: 145 us
  blocking collectives  57.9 us (40%)
  waiting for transfers between devices  45.4 us (31%)
  other arithmetic  18.6 us (13%)
  between operations  13.6 us (9%)
  starting transfers between devices  7.13 us (5%)
  local copies, waits for them, and re-layouts  2.91 us (2%)
    reduce_scatter x2, waiting for transfers between devices, per_device(): lax.psum_scatter(term, 'freq', scatter_dimension=0, tiled=True)  41.9 us
    all_gather x2, blocking collectives, per_device(): lax.all_gather(velocity[depth], 'freq', axis=0, tiled=True)  30.2 us
    all_gather x2, blocking collectives, per_device(): lax.all_gather(eta[depth], 'freq', axis=0, tiled=True)  27.7 us
    add x2, other arithmetic, stencil(): total = total + weight * part  5.84 us
    ppermute x2, starting transfers between devices, with_halo(): lax.ppermute(tail, axis, [(i, (i + 1) % count) for i in range(ends)])  4.32 us
    cos x1, other arithmetic, advance(): cosine = jnp.cos(phase)  3.7 us
    ppermute x2, waiting for transfers between devices, with_halo(): lax.ppermute(head, axis, [((i + 1) % count, i) for i in range(ends)])  3.46 us
  transfers between devices with their start and end apart: 6, of which 3 were waited for; matrix products, arithmetic and copies ran while one was open for 5% of the time, Pallas kernels for 0%

commit v1 on v0

v1 whole, which is shorter than its diff:
```python
import functools

import jax
import jax.numpy as jnp
from jax import lax
from jax.experimental import pallas as pl
from jax.experimental.pallas import tpu as pltpu
from jax.sharding import PartitionSpec as P

MESH = pl.DeviceIdType.MESH
PAD = 16
HALO = 8

CENTRE = -980.0
WEIGHTS = ((1, 135.0), (2, -13.5), (3, 1.0))


def band(distance, centre):
    out = jnp.where(distance == 0, centre, 0.0)
    for shift, weight in WEIGHTS:
        out = jnp.where(jnp.abs(distance) == shift, weight, out)
    return out.astype(jnp.bfloat16)


def cos_sin(x):
    z = x * x
    c = -1.0 / 3628800.0
    for k in (1.0 / 40320.0, -1.0 / 720.0, 1.0 / 24.0, -0.5, 1.0):
        c = c * z + k
    s = 1.0 / 362880.0
    for k in (-1.0 / 5040.0, 1.0 / 120.0, -1.0 / 6.0, 1.0):
        s = s * z + k
    return c, s * x


def kernel(n, tiles, omega_ref, wf, vel, eta, out, a_buf, b_buf, va, term, rbuf,
           my_buf, mx_buf, local_sem, zs, zr, ys, yr, hs, hr, rs, rr):
    depths = vel.shape[0]
    shard = vel.shape[1]
    rows, cols = wf.shape[3], wf.shape[4]
    freqs = wf.shape[2]
    me = lax.axis_index("freq")
    shot = lax.axis_index("shot")
    tile = lax.axis_index("tile")
    other = 1 - shot
    has_up = tile > 0
    has_down = tile < tiles - 1

    def rows_of(o):
        return pl.ds(pl.multiple_of(o * shard, shard), shard)

    load_v = pltpu.make_async_copy(vel, va.at[0, :, rows_of(me)], local_sem.at[0])
    load_e = pltpu.make_async_copy(eta, va.at[1, :, rows_of(me)], local_sem.at[1])
    load_f = pltpu.make_async_copy(wf, a_buf.at[:, :, :, pl.ds(PAD, rows)], local_sem.at[2])
    load_v.start()
    load_e.start()
    load_f.start()

    barrier = pltpu.get_barrier_semaphore()

    def greet(k, carry):
        @pl.when(k != me)
        def _():
            pl.semaphore_signal(barrier, inc=1, device_id={"freq": k}, device_id_type=MESH)
        return carry

    lax.fori_loop(0, n, greet, 0)
    pl.semaphore_signal(barrier, inc=1, device_id={"shot": other}, device_id_type=MESH)

    @pl.when(has_up)
    def _():
        pl.semaphore_signal(barrier, inc=1, device_id={"tile": tile - 1}, device_id_type=MESH)

    @pl.when(has_down)
    def _():
        pl.semaphore_signal(barrier, inc=1, device_id={"tile": tile + 1}, device_id_type=MESH)

    r = lax.broadcasted_iota(jnp.int32, (cols, cols), 0)
    c = lax.broadcasted_iota(jnp.int32, (cols, cols), 1)
    my = band(r - c, CENTRE)
    my_buf[0:cols] = my
    my_buf[cols:2 * cols] = my
    window = shard + 2 * PAD
    r = lax.broadcasted_iota(jnp.int32, (shard, window), 0)
    c = lax.broadcasted_iota(jnp.int32, (shard, window), 1)
    mx_buf[:, 0:window] = band(c - PAD - r, 0.0)
    for buf in (a_buf, b_buf):
        zeros = jnp.zeros(buf.shape[:3] + (PAD - HALO, cols), jnp.float32)
        buf[:, :, :, 0:PAD - HALO] = zeros
        buf[:, :, :, PAD + rows + HALO:2 * PAD + rows] = zeros

        @pl.when(jnp.logical_not(has_up))
        def _():
            buf[:, :, :, PAD - HALO:PAD] = jnp.zeros(buf.shape[:3] + (HALO, cols), jnp.float32)

        @pl.when(jnp.logical_not(has_down))
        def _():
            buf[:, :, :, PAD + rows:PAD + rows + HALO] = jnp.zeros(buf.shape[:3] + (HALO, cols), jnp.float32)

    pl.semaphore_wait(barrier, n + has_up.astype(jnp.int32) + has_down.astype(jnp.int32))

    def halo(d, slot):
        if d == 0:
            src = wf.at[:, :, :, pl.ds(0 if slot == 0 else rows - HALO, HALO)]
            buf = a_buf
        else:
            src = b_buf.at[:, :, :, pl.ds(PAD if slot == 0 else PAD + rows - HALO, HALO)]
            buf = b_buf
        dst = buf.at[:, :, :, pl.ds(PAD + rows if slot == 0 else PAD - HALO, HALO)]
        return pltpu.make_async_remote_copy(
            src_ref=src, dst_ref=dst, send_sem=hs.at[d, slot], recv_sem=hr.at[d, slot],
            device_id={"tile": tile - 1 if slot == 0 else tile + 1}, device_id_type=MESH)

    def on_line(d, o, way):
        slot = va.at[shot, d, rows_of(o)]
        return pltpu.make_async_remote_copy(
            src_ref=slot, dst_ref=slot, send_sem=zs.at[way, d, o], recv_sem=zr.at[d, o],
            device_id={"freq": me + 1 if way else me - 1}, device_id_type=MESH)

    def across(d, o, which):
        slot = va.at[which, d, rows_of(o)]
        return pltpu.make_async_remote_copy(
            src_ref=slot, dst_ref=slot, send_sem=ys.at[d, o], recv_sem=yr.at[d, o],
            device_id={"shot": other}, device_id_type=MESH)

    def summand(d, to, frm):
        return pltpu.make_async_remote_copy(
            src_ref=term.at[d, rows_of(to)], dst_ref=rbuf.at[d, rows_of(frm)],
            send_sem=rs.at[d, to], recv_sem=rr.at[d, frm],
            device_id={"freq": to}, device_id_type=MESH)

    def send_own(d):
        @pl.when(me < n - 1)
        def _():
            on_line(d, me, 1).start()

        @pl.when(me > 0)
        def _():
            on_line(d, me, 0).start()

    def pass_on(d, dist):
        low, high = me - dist, me + dist

        @pl.when(low >= 0)
        def _():
            on_line(d, low, 1).wait_recv()

            @pl.when(me < n - 1)
            def _():
                on_line(d, low, 1).start()
            across(d, low, shot).start()

        @pl.when(high < n)
        def _():
            on_line(d, high, 0).wait_recv()

            @pl.when(me > 0)
            def _():
                on_line(d, high, 0).start()
            across(d, high, shot).start()

    mesh_rows = (shard, cols)

    def block(d, o, src, dst):
        start = pl.multiple_of(o * shard, shard)
        v = va[0, d, pl.ds(start, shard)]
        e = va[1, d, pl.ds(start, shard)]
        inv = 1.0 / v
        lift = v * (1.0 + 2.0 * e) * (0.5 / 90.0)
        mx = mx_buf[:, 0:window]
        mx2 = jnp.concatenate([mx, mx], axis=1)
        total = None
        for w in range(freqs):
            om = jnp.full((1, cols), omega_ref[w], jnp.float32)
            theta = lift * (1.0 / om)
            cosine, sine = cos_sin(inv * (om * 0.01))
            mids, along, lhs = [], [], []
            for s in range(2):
                for k in range(2):
                    f = src[s, k, w, pl.ds(start, window)]
                    hi = f.astype(jnp.bfloat16)
                    lo = (f - hi.astype(jnp.float32)).astype(jnp.bfloat16)
                    mids.append(f[PAD:PAD + shard])
                    along.append(jnp.dot(mx2, jnp.concatenate([hi, lo], axis=0),
                                         preferred_element_type=jnp.float32))
                    lhs.append(jnp.concatenate([hi[PAD:PAD + shard], lo[PAD:PAD + shard]], axis=1))
            ydir = jnp.dot(jnp.concatenate(lhs, axis=0), my_buf[...], preferred_element_type=jnp.float32)
            laps = [along[i] + ydir[i * shard:(i + 1) * shard] for i in range(4)]
            outs = []
            for s in range(2):
                sign = -1.0 if s == 0 else 1.0
                re, im = mids[2 * s], mids[2 * s + 1]
                lre, lim = theta * laps[2 * s], theta * laps[2 * s + 1]
                if s == 0:
                    vre, vim = re + lim, im - lre
                    ore = cosine * vre + sine * vim
                    oim = cosine * vim - sine * vre
                else:
                    vre, vim = re - lim, im + lre
                    ore = cosine * vre - sine * vim
                    oim = cosine * vim + sine * vre
                outs.append((ore, oim))
                if dst is not None:
                    at = pl.ds(pl.multiple_of(start + PAD, 8), shard)
                    dst[s, 0, w, at] = ore
                    dst[s, 1, w, at] = oim
            part = outs[0][0] * outs[1][0] + outs[0][1] * outs[1][1]
            total = part if total is None else total + part
        term[d, pl.ds(start, shard)] = total

        @pl.when(o != me)
        def _():
            summand(d, o, me).start()

    @pl.when(has_up)
    def _():
        halo(0, 0).start()

    @pl.when(has_down)
    def _():
        halo(0, 1).start()

    load_v.wait()
    load_e.wait()
    send_own(0)
    load_f.wait()

    def halo_wait(d, o):
        @pl.when(jnp.logical_and(o == 0, has_up))
        def _():
            halo(d, 1).wait_recv()

        @pl.when(jnp.logical_and(o == n - 1, has_down))
        def _():
            halo(d, 0).wait_recv()

    def first(s, carry):
        @pl.when(s < n)
        def _():
            pass_on(0, s)

        @pl.when(s == 1)
        def _():
            for d in range(1, depths):
                send_own(d)

        @pl.when(s > 1)
        def _():
            for d in range(1, depths):
                pass_on(d, s - 1)

        def one(way, carry):
            o = jnp.where(way == 0, me - (s - 1), me + (s - 1))

            @pl.when(jnp.logical_and(jnp.logical_and(o >= 0, o < n),
                                     jnp.logical_or(way == 0, s > 1)))
            def _():
                @pl.when(s > 1)
                def _():
                    across(0, o, other).wait_recv()
                halo_wait(0, o)
                block(0, o, a_buf, b_buf)

                @pl.when(jnp.logical_and(o == 0, has_up))
                def _():
                    halo(1, 0).start()

                @pl.when(jnp.logical_and(o == n - 1, has_down))
                def _():
                    halo(1, 1).start()
            return carry

        lax.fori_loop(0, 2, one, 0)
        return carry

    lax.fori_loop(1, n + 1, first, 0)

    def second(i, carry):
        o = jnp.where(i < n - 2, i + 1, jnp.where(i == n - 2, 0, n - 1))

        @pl.when(o != me)
        def _():
            across(1, o, other).wait_recv()
        halo_wait(1, o)
        block(1, o, b_buf, None)
        return carry

    lax.fori_loop(0, n, second, 0)

    for d in range(depths):
        total = term[d, rows_of(me)]

        def add(k, total):
            o = lax.rem(me + k, n)
            summand(d, o, o).wait_recv()
            return total + rbuf[d, rows_of(o)]

        out[d] = lax.fori_loop(1, n, add, total)

    for d in range(depths):
        @pl.when(has_up)
        def _():
            halo(d, 0).wait_send()

        @pl.when(has_down)
        def _():
            halo(d, 1).wait_send()

        def drain(o, carry):
            @pl.when(jnp.logical_and(o <= me, me < n - 1))
            def _():
                on_line(d, o, 1).wait_send()

            @pl.when(jnp.logical_and(o >= me, me > 0))
            def _():
                on_line(d, o, 0).wait_send()

            @pl.when(o != me)
            def _():
                across(d, o, shot).wait_send()
                summand(d, o, me).wait_send()
            return carry

        lax.fori_loop(0, n, drain, 0)


def per_device(n, tiles, omega, wavefields, velocity, eta):
    depths, shard, cols = velocity.shape
    sides, parts, freqs, rows, _ = wavefields.shape
    padded = (sides, parts, freqs, rows + 2 * PAD, cols)
    dma = pltpu.SemaphoreType.DMA
    return pl.pallas_call(
        functools.partial(kernel, n, tiles),
        out_shape=jax.ShapeDtypeStruct((depths, shard, cols), jnp.float32),
        in_specs=[pl.BlockSpec(memory_space=pltpu.SMEM)] + [pl.BlockSpec(memory_space=pl.ANY)] * 3,
        out_specs=pl.BlockSpec(memory_space=pltpu.VMEM),
        scratch_shapes=[
            pltpu.VMEM(padded, jnp.float32),
            pltpu.VMEM(padded, jnp.float32),
            pltpu.VMEM((2, depths, rows, cols), jnp.float32),
            pltpu.VMEM((depths, rows, cols), jnp.float32),
            pltpu.VMEM((depths, rows, cols), jnp.float32),
            pltpu.VMEM((2 * cols, cols), jnp.bfloat16),
            pltpu.VMEM((shard, shard + 2 * PAD), jnp.bfloat16),
            dma((3,)),
            dma((2, depths, n)),
            dma((depths, n)),
            dma((depths, n)),
            dma((depths, n)),
            dma((depths, 2)),
            dma((depths, 2)),
            dma((depths, n)),
            dma((depths, n)),
        ],
        compiler_params=pltpu.CompilerParams(
            collective_id=0, has_side_effects=True, vmem_limit_bytes=40 * 1024 * 1024),
    )(omega, wavefields, velocity, eta)


def solution(mesh):
    return jax.shard_map(
        functools.partial(per_device, mesh.shape["freq"], mesh.shape["tile"]),
        mesh=mesh,
        in_specs=(
            P("freq"),
            P("shot", None, "freq", "tile", None),
            P(None, ("tile", "freq"), None),
            P(None, ("tile", "freq"), None),
        ),
        out_specs=P("shot", ("tile", "freq"), None),
        check_vma=False,
    )
```

time: 146 us -> 33.5 us (0.23)
  blocking collectives: 57.9 us -> 0 us
  waiting for transfers between devices: 45.4 us -> 0 us
  Pallas kernels: 0 us -> 28.6 us
  other arithmetic: 18.6 us -> 0 us
  between operations: 13.6 us -> 0.01 us
  starting transfers between devices: 7.13 us -> 0 us
  local copies, waits for them, and re-layouts: 2.91 us -> 4.71 us
    all_gather x4 -> x0, blocking collectives: 57.9 us -> none  [the longest x2 30.2 us: per_device(): lax.all_gather(velocity[depth], 'freq', axis=0, tiled=True)]
    reduce_scatter x2 -> x0, waiting for transfers between devices: 41.9 us -> none  [per_device(): lax.psum_scatter(term, 'freq', scatter_dimension=0, tiled=True)]
    pallas_call x0 -> x1, Pallas kernels: none -> 28.6 us  [per_device(): pl.pallas_call(functools.partial(kernel, n, tiles), out_shape=jax.ShapeDt...]
    ppermute x4 -> x0, starting transfers between devices: 7.09 us -> none  [the longest x2 4.32 us: with_halo(): lax.ppermute(tail, axis, [(i, (i + 1) % count) for i in range(ends)])]
    add x4 -> x0, other arithmetic: 6.91 us -> none  [the longest x2 5.84 us: stencil(): total = total + weight * part]
    unnamed x7 -> x9, local copies, waits for them, and re-layouts: 0.23 us -> 4.71 us
    cos x1 -> x0, other arithmetic: 3.7 us -> none  [advance(): cosine = jnp.cos(phase)]
    ppermute x4 -> x0, waiting for transfers between devices: 3.46 us -> none  [the longest x2 3.46 us: with_halo(): lax.ppermute(head, axis, [((i + 1) % count, i) for i in range(ends)])]
  transfers between devices with their start and end apart: 6 -> 0, of which waited for: 3 -> 0; matrix products, arithmetic and copies ran while one was open for 5% -> 0% of each run, Pallas kernels for 0% -> 0%
where the time goes in v1:
time: 33.5 us; the launch traced here: 33.3 us
  Pallas kernels  28.6 us (85%)
  local copies, waits for them, and re-layouts  4.71 us (14%)
    pallas_call x1, Pallas kernels, per_device(): pl.pallas_call(functools.partial(kernel, n, tiles), out_shape=jax.ShapeDt...  28.6 us
    unnamed x9, local copies, waits for them, and re-layouts  4.71 us

profile of v1, /device:TPU:0, one launch (start us, length us, event | category | flops | bytes accessed | tf_op | source)
XLA Modules:
  0.0 33.3 jit_solution(10180719897798030532)
XLA Ops:
  0.0 0.0 copy-start
  0.0 1.6 %copy-done = f32[2,2,2,256,256]{4,3,2,1,0:T(8,128)S(1)} copy-done((f32[2,2,2,256,256]{4,3,2,1,0:T(8,128)S(1)}, f32[2,2,2,256,256]{4,3,2,1,0:T(8,128)}, u32[]{:S(2)}) %copy-start) | copy-done | bytes 2097176
  1.6 0.0 copy-start.1
  1.6 0.9 %copy-done.1 = f32[2,64,256]{2,1,0:T(8,128)S(1)} copy-done((f32[2,64,256]{2,1,0:T(8,128)S(1)}, f32[2,64,256]{2,1,0:T(8,128)}, u32[]{:S(2)}) %copy-start.1) | copy-done | bytes 131096
  2.5 0.0 copy-start.2
  2.5 0.9 %copy-done.2 = f32[2,64,256]{2,1,0:T(8,128)S(1)} copy-done((f32[2,64,256]{2,1,0:T(8,128)S(1)}, f32[2,64,256]{2,1,0:T(8,128)}, u32[]{:S(2)}) %copy-start.2) | copy-done | bytes 131096
  3.4 0.0 copy-start.3
  3.4 0.7 %copy-done.3 = f32[2]{0:T(128)S(1)} copy-done((f32[2]{0:T(128)S(1)}, f32[2]{0:T(128)}, u32[]{:S(2)}) %copy-start.3) | copy-done | bytes 32
  4.1 28.6 %shard_map.46 = f32[2,64,256]{2,1,0:T(8,128)S(1)} custom-call(f32[2]{0:T(128)S(1)} %copy-done.3, f32[2,2,2,256,256]{4,3,2,1,0:T(8,128)S(1)} %copy-done, f32[2,64,256]{2,1,0:T(8,128)S(1)} %copy-done.1, f32[2,64,256]{2,1,0:T(8,128)S(1)} %copy-done.2), custom_call_target="tpu_custom_call" | custom-call | tf_op jit(solution)/shard_map/pallas_call | solution.py:332
  32.7 0.7 %copy.6 = f32[2,64,256]{2,1,0:T(8,128)} copy(f32[2,64,256]{2,1,0:T(8,128)S(1)} %shard_map.46) | data formatting | bytes 262144
Async XLA Ops:
  0.0 1.6 %copy-start = (f32[2,2,2,256,256]{4,3,2,1,0:T(8,128)S(1)}, f32[2,2,2,256,256]{4,3,2,1,0:T(8,128)}, u32[]{:S(2)}) copy-start(f32[2,2,2,256,256]{4,3,2,1,0:T(8,128)} %wf.1) | copy-start | bytes 6291460
  1.6 0.9 %copy-start.1 = (f32[2,64,256]{2,1,0:T(8,128)S(1)}, f32[2,64,256]{2,1,0:T(8,128)}, u32[]{:S(2)}) copy-start(f32[2,64,256]{2,1,0:T(8,128)} %vel.1) | copy-start | bytes 393220
  2.5 0.9 %copy-start.2 = (f32[2,64,256]{2,1,0:T(8,128)S(1)}, f32[2,64,256]{2,1,0:T(8,128)}, u32[]{:S(2)}) copy-start(f32[2,64,256]{2,1,0:T(8,128)} %eta.1) | copy-start | bytes 393220
  3.4 0.7 %copy-start.3 = (f32[2]{0:T(128)S(1)}, f32[2]{0:T(128)}, u32[]{:S(2)}) copy-start(f32[2]{0:T(128)} %omega_ref.1) | copy-start | bytes 28

commit v2 on v1

--- a/solution.py
+++ b/solution.py
@@ -8,6 +8,9 @@
 from jax.sharding import PartitionSpec as P
 
 MESH = pl.DeviceIdType.MESH
+CHAINED = ()
+DIRECT = ()
+EARLY = False
 PAD = 16
 HALO = 8
 
@@ -33,8 +36,8 @@
     return c, s * x
 
 
-def kernel(n, tiles, omega_ref, wf, vel, eta, out, a_buf, b_buf, va, term, rbuf,
-           my_buf, mx_buf, local_sem, zs, zr, ys, yr, hs, hr, rs, rr):
+def kernel(n, tiles, omega_hbm, wf, vel, eta, out, a_buf, b_buf, va, term, rbuf, cbuf,
+           my_buf, mx_buf, omega_ref, local_sem, zs, zr, ys, yr, hs, hr, rs, rr, cr):
     depths = vel.shape[0]
     shard = vel.shape[1]
     rows, cols = wf.shape[3], wf.shape[4]
@@ -52,9 +55,11 @@
     load_v = pltpu.make_async_copy(vel, va.at[0, :, rows_of(me)], local_sem.at[0])
     load_e = pltpu.make_async_copy(eta, va.at[1, :, rows_of(me)], local_sem.at[1])
     load_f = pltpu.make_async_copy(wf, a_buf.at[:, :, :, pl.ds(PAD, rows)], local_sem.at[2])
+    load_o = pltpu.make_async_copy(omega_hbm, omega_ref, local_sem.at[3])
     load_v.start()
     load_e.start()
     load_f.start()
+    load_o.start()
 
     barrier = pltpu.get_barrier_semaphore()
 
@@ -129,37 +134,63 @@
             send_sem=rs.at[d, to], recv_sem=rr.at[d, frm],
             device_id={"freq": to}, device_id_type=MESH)
 
+    def chain(d, o, way):
+        return pltpu.make_async_remote_copy(
+            src_ref=term.at[d, rows_of(o)], dst_ref=cbuf.at[way, d, rows_of(o)],
+            send_sem=rs.at[d, o], recv_sem=cr.at[way, d, o],
+            device_id={"freq": me + 1 if way else me - 1}, device_id_type=MESH)
+
+    def relay(d, pos):
+        def step(k, carry):
+            for way, first in ((1, me == pos), (0, n - 1 - me == pos)):
+                o = me + k if way else me - k
+
+                @pl.when(jnp.logical_and(first, jnp.logical_and(o >= 0, o < n)))
+                def _():
+                    chain(d, o, way).wait_recv()
+                    term[d, rows_of(o)] += cbuf[way, d, rows_of(o)]
+                    chain(d, o, way).start()
+            return carry
+
+        lax.fori_loop(1, n, step, 0)
+
+    def to_all(d, to):
+        slot = va.at[shot, d, rows_of(me)]
+        return pltpu.make_async_remote_copy(
+            src_ref=slot, dst_ref=slot, send_sem=zs.at[0, d, to], recv_sem=zr.at[d, me],
+            device_id={"freq": to}, device_id_type=MESH)
+
     def send_own(d):
-        @pl.when(me < n - 1)
-        def _():
-            on_line(d, me, 1).start()
-
-        @pl.when(me > 0)
-        def _():
-            on_line(d, me, 0).start()
+        if d in DIRECT:
+            def step(k, carry):
+                for to in (me + k, me - k):
+                    @pl.when(jnp.logical_and(to >= 0, to < n))
+                    def _():
+                        to_all(d, to).start()
+                return carry
+
+            lax.fori_loop(1, n, step, 0)
+        else:
+            @pl.when(me < n - 1)
+            def _():
+                on_line(d, me, 1).start()
+
+            @pl.when(me > 0)
+            def _():
+                on_line(d, me, 0).start()
 
     def pass_on(d, dist):
-        low, high = me - dist, me + dist
-
-        @pl.when(low >= 0)
-        def _():
-            on_line(d, low, 1).wait_recv()
-
-            @pl.when(me < n - 1)
-            def _():
-                on_line(d, low, 1).start()
-            across(d, low, shot).start()
-
-        @pl.when(high < n)
-        def _():
-            on_line(d, high, 0).wait_recv()
-
-            @pl.when(me > 0)
-            def _():
-                on_line(d, high, 0).start()
-            across(d, high, shot).start()
-
-    mesh_rows = (shard, cols)
+        for way in (1, 0):
+            o = me - dist if way else me + dist
+
+            @pl.when(jnp.logical_and(o >= 0, o < n))
+            def _():
+                on_line(d, o, way).wait_recv()
+                if d not in DIRECT:
+                    @pl.when(me < n - 1 if way else me > 0)
+                    def _():
+                        on_line(d, o, way).start()
+                across(d, o, shot).start()
 
     def block(d, o, src, dst):
         start = pl.multiple_of(o * shard, shard)
@@ -208,9 +239,18 @@
             total = part if total is None else total + part
         term[d, pl.ds(start, shard)] = total
 
-        @pl.when(o != me)
-        def _():
-            summand(d, o, me).start()
+        if d in CHAINED:
+            @pl.when(jnp.logical_and(o > me, me == 0))
+            def _():
+                chain(d, o, 1).start()
+
+            @pl.when(jnp.logical_and(o < me, me == n - 1))
+            def _():
+                chain(d, o, 0).start()
+        else:
+            @pl.when(o != me)
+            def _():
+                summand(d, o, me).start()
 
     @pl.when(has_up)
     def _():
@@ -223,7 +263,11 @@
     load_v.wait()
     load_e.wait()
     send_own(0)
+    if EARLY:
+        for d in range(1, depths):
+            send_own(d)
     load_f.wait()
+    load_o.wait()
 
     def halo_wait(d, o):
         @pl.when(jnp.logical_and(o == 0, has_up))
@@ -239,23 +283,24 @@
         def _():
             pass_on(0, s)
 
-        @pl.when(s == 1)
-        def _():
-            for d in range(1, depths):
-                send_own(d)
-
-        @pl.when(s > 1)
+        if not EARLY:
+            @pl.when(s == 1)
+            def _():
+                for d in range(1, depths):
+                    send_own(d)
+
+        @pl.when(jnp.logical_and(s > 1, s <= n))
         def _():
             for d in range(1, depths):
                 pass_on(d, s - 1)
 
         def one(way, carry):
-            o = jnp.where(way == 0, me - (s - 1), me + (s - 1))
+            o = jnp.where(way == 0, me - (s - 2), me + (s - 2))
 
             @pl.when(jnp.logical_and(jnp.logical_and(o >= 0, o < n),
-                                     jnp.logical_or(way == 0, s > 1)))
-            def _():
-                @pl.when(s > 1)
+                                     jnp.logical_and(s >= 2, jnp.logical_or(way == 0, s > 2))))
+            def _():
+                @pl.when(s > 2)
                 def _():
                     across(0, o, other).wait_recv()
                 halo_wait(0, o)
@@ -273,29 +318,52 @@
         lax.fori_loop(0, 2, one, 0)
         return carry
 
-    lax.fori_loop(1, n + 1, first, 0)
+    lax.fori_loop(1, n + 2, first, 0)
 
     def second(i, carry):
         o = jnp.where(i < n - 2, i + 1, jnp.where(i == n - 2, 0, n - 1))
+        o = jnp.where(2 * me < n, o, n - 1 - o)
 
         @pl.when(o != me)
         def _():
             across(1, o, other).wait_recv()
         halo_wait(1, o)
         block(1, o, b_buf, None)
+
+        if 0 in CHAINED:
+            @pl.when(i > 0)
+            def _():
+                relay(0, i)
         return carry
 
     lax.fori_loop(0, n, second, 0)
 
+    for d in range(1, depths):
+        if d in CHAINED:
+            for pos in range(1, n - 1):
+                relay(d, pos)
     for d in range(depths):
-        total = term[d, rows_of(me)]
-
-        def add(k, total):
-            o = lax.rem(me + k, n)
-            summand(d, o, o).wait_recv()
-            return total + rbuf[d, rows_of(o)]
-
-        out[d] = lax.fori_loop(1, n, add, total)
+        if d in CHAINED:
+            out[d] = term[d, rows_of(me)]
+
+            @pl.when(me > 0)
+            def _():
+                chain(d, me, 1).wait_recv()
+                out[d] += cbuf[1, d, rows_of(me)]
+
+            @pl.when(me < n - 1)
+            def _():
+                chain(d, me, 0).wait_recv()
+                out[d] += cbuf[0, d, rows_of(me)]
+        else:
+            total = term[d, rows_of(me)]
+
+            def add(k, total):
+                o = lax.rem(me + k, n)
+                summand(d, o, o).wait_recv()
+                return total + rbuf[d, rows_of(o)]
+
+            out[d] = lax.fori_loop(1, n, add, total)
 
     for d in range(depths):
         @pl.when(has_up)
@@ -307,18 +375,21 @@
             halo(d, 1).wait_send()
 
         def drain(o, carry):
-            @pl.when(jnp.logical_and(o <= me, me < n - 1))
-            def _():
-                on_line(d, o, 1).wait_send()
-
-            @pl.when(jnp.logical_and(o >= me, me > 0))
-            def _():
-                on_line(d, o, 0).wait_send()
+            if d not in DIRECT:
+                @pl.when(jnp.logical_and(o <= me, me < n - 1))
+                def _():
+                    on_line(d, o, 1).wait_send()
+
+                @pl.when(jnp.logical_and(o >= me, me > 0))
+                def _():
+                    on_line(d, o, 0).wait_send()
 
             @pl.when(o != me)
             def _():
+                if d in DIRECT:
+                    to_all(d, o).wait_send()
                 across(d, o, shot).wait_send()
-                summand(d, o, me).wait_send()
+                chain(d, o, 1).wait_send()
             return carry
 
         lax.fori_loop(0, n, drain, 0)
@@ -332,7 +403,7 @@
     return pl.pallas_call(
         functools.partial(kernel, n, tiles),
         out_shape=jax.ShapeDtypeStruct((depths, shard, cols), jnp.float32),
-        in_specs=[pl.BlockSpec(memory_space=pltpu.SMEM)] + [pl.BlockSpec(memory_space=pl.ANY)] * 3,
+        in_specs=[pl.BlockSpec(memory_space=pltpu.HBM)] * 4,
         out_specs=pl.BlockSpec(memory_space=pltpu.VMEM),
         scratch_shapes=[
             pltpu.VMEM(padded, jnp.float32),
@@ -340,9 +411,11 @@
             pltpu.VMEM((2, depths, rows, cols), jnp.float32),
             pltpu.VMEM((depths, rows, cols), jnp.float32),
             pltpu.VMEM((depths, rows, cols), jnp.float32),
+            pltpu.VMEM((2, depths, rows, cols), jnp.float32),
             pltpu.VMEM((2 * cols, cols), jnp.bfloat16),
             pltpu.VMEM((shard, shard + 2 * PAD), jnp.bfloat16),
-            dma((3,)),
+            pltpu.SMEM((freqs,), jnp.float32),
+            dma((4,)),
             dma((2, depths, n)),
             dma((depths, n)),
             dma((depths, n)),
@@ -351,9 +424,10 @@
             dma((depths, 2)),
             dma((depths, n)),
             dma((depths, n)),
+            dma((2, depths, n)),
         ],
         compiler_params=pltpu.CompilerParams(
-            collective_id=0, has_side_effects=True, vmem_limit_bytes=40 * 1024 * 1024),
+            collective_id=0, has_side_effects=True, vmem_limit_bytes=63 * 1024 * 1024),
     )(omega, wavefields, velocity, eta)
 
 

time: 33.5 us -> 30.9 us (0.922)
  local copies, waits for them, and re-layouts: 4.71 us -> 1.57 us
    unnamed x9 -> x1, local copies, waits for them, and re-layouts: 4.71 us -> 1.57 us
where the time goes in v2:
time: 30.9 us; the launch traced here: 30.4 us
  Pallas kernels  28.9 us (94%)
  local copies, waits for them, and re-layouts  1.57 us (5%)
    pallas_call x1, Pallas kernels, per_device(): pl.pallas_call(functools.partial(kernel, n, tiles), out_shape=jax.ShapeDt...  28.9 us
    unnamed x1, local copies, waits for them, and re-layouts  1.57 us

profile of v2, /device:TPU:0, one launch (start us, length us, event | category | flops | bytes accessed | tf_op | source)
XLA Modules:
  0.0 30.4 jit_solution(11081455767896285278)
XLA Ops:
  0.0 28.9 %shard_map.46 = f32[2,64,256]{2,1,0:T(8,128)} custom-call(f32[2]{0:T(128)} %omega_hbm.1, f32[2,2,2,256,256]{4,3,2,1,0:T(8,128)} %wf.1, f32[2,64,256]{2,1,0:T(8,128)} %vel.1, f32[2,64,256]{2,1,0:T(8,128)} %eta.1), custom_call_target="tpu_custom_call" | custom-call | tf_op jit(solution)/shard_map/pallas_call | solution.py:403
  28.9 1.6 %copy.6 = f32[2,64,256]{2,1,0:T(8,128)} copy(f32[2,64,256]{2,1,0:T(8,128)} %shard_map.46) | data formatting | bytes 262144

commit v3 on v2

--- a/solution.py
+++ b/solution.py
@@ -186,11 +186,11 @@
             @pl.when(jnp.logical_and(o >= 0, o < n))
             def _():
                 on_line(d, o, way).wait_recv()
+                across(d, o, shot).start()
                 if d not in DIRECT:
                     @pl.when(me < n - 1 if way else me > 0)
                     def _():
                         on_line(d, o, way).start()
-                across(d, o, shot).start()
 
     def block(d, o, src, dst):
         start = pl.multiple_of(o * shard, shard)
@@ -252,20 +252,20 @@
             def _():
                 summand(d, o, me).start()
 
-    @pl.when(has_up)
-    def _():
-        halo(0, 0).start()
-
-    @pl.when(has_down)
-    def _():
-        halo(0, 1).start()
-
     load_v.wait()
     load_e.wait()
     send_own(0)
     if EARLY:
         for d in range(1, depths):
             send_own(d)
+    @pl.when(has_up)
+    def _():
+        halo(0, 0).start()
+
+    @pl.when(has_down)
+    def _():
+        halo(0, 1).start()
+
     load_f.wait()
     load_o.wait()
 

time: 30.9 us -> 30.9 us (level)
  no operation moved by 1% of the time
where the time goes in v3:
time: 30.9 us; the launch traced here: 30.5 us
  Pallas kernels  28.9 us (94%)
  local copies, waits for them, and re-layouts  1.57 us (5%)
    pallas_call x1, Pallas kernels, per_device(): pl.pallas_call(functools.partial(kernel, n, tiles), out_shape=jax.ShapeDt...  28.9 us
    unnamed x1, local copies, waits for them, and re-layouts  1.57 us

profile of v3, /device:TPU:0, one launch (start us, length us, event | category | flops | bytes accessed | tf_op | source)
XLA Modules:
  0.0 30.5 jit_solution(3497158346650223596)
XLA Ops:
  0.0 28.9 %shard_map.46 = f32[2,64,256]{2,1,0:T(8,128)} custom-call(f32[2]{0:T(128)} %omega_hbm.1, f32[2,2,2,256,256]{4,3,2,1,0:T(8,128)} %wf.1, f32[2,64,256]{2,1,0:T(8,128)} %vel.1, f32[2,64,256]{2,1,0:T(8,128)} %eta.1), custom_call_target="tpu_custom_call" | custom-call | tf_op jit(solution)/shard_map/pallas_call | solution.py:403
  28.9 1.6 %copy.6 = f32[2,64,256]{2,1,0:T(8,128)} copy(f32[2,64,256]{2,1,0:T(8,128)} %shard_map.46) | data formatting | bytes 262144
